TPU v7x, 256 devices: a whole 4x4x8 slice. The times are simulated.
256 devices in a mesh: frames: 64 (over y, x_hi, z), heads: 4 (over x_lo, core).
Axes of the slice: x: 4 (x_hi: 2, x_lo: 2; x = x_hi * 2 + x_lo), y: 4, z: 8, core: 2. Of those that a mesh axis runs over, the one named last changes fastest.
Arguments:
- span_q: bfloat16 [32768, 5120], P('frames', 'heads'), may hold values from -6 to 6
- span_k: bfloat16 [32768, 5120], P('frames', 'heads'), may hold values from -6 to 6
- span_v: bfloat16 [32768, 5120], P('frames', 'heads'), may hold values from -6 to 6
- q_gain: float32 [5120], P('heads'), may hold values from 1 to 3
- k_gain: float32 [5120], P('heads'), may hold values from 0.5 to 2
- kv_cache: bfloat16 [128, 2, 128, 5120], P('frames', None, None, 'heads'), may hold values from -6 to 6
- frame_home: int32 [128], replicated, may hold values from 0 to 127, each once
- chosen_frames: int32 [5], replicated, may hold values from 0 to 127, as said below
Outputs:
- attended: bfloat16 [32768, 5120], P('frames', 'heads')
Inputs may be any that keep to these rules, and one draw needn't show every extreme that they name: A permutation: frame i of the history is kept in row frame_home[i] of kv_cache. `chosen_frames`: 2 distinct key frames below 125, then the 3 most recent frames 128 - 3 to 127 in order.
All inputs are finite; a program needn't handle non-finite values.
Results may differ from a plain program's by a relative error of at most 0.012.
Values may be sent and summed in bfloat16 or wider, within the bound.
No kernel may reach another device: no remote copies, remote signals or barrier semaphores. Data moves between devices by JAX's collectives and lax.ppermute only.
A program may use at most 128 MiB of HBM per device.

v0:
```python
import math

import jax
import jax.numpy as jnp
from jax import lax
from jax.sharding import PartitionSpec as P

D = 5120
HD = 128
GROUP = 8
SEL = 5


logit_cap = 30.0


def partner(value, axis, apart):
    return lax.ppermute(value, axis, [(i, i ^ 1 << apart) for i in range(lax.axis_size(axis))])


def from_root(block, axis, source):
    block = jnp.where(lax.axis_index(axis) == source, block, jnp.zeros_like(block))
    return lax.psum(block, axis)


def partial_sums(queries, keys_here, values_here):
    row_total = queries.shape[0]
    key_total = keys_here.shape[0]
    feature_width = queries.shape[1]
    head_total = feature_width // HD
    query_heads = queries.reshape(row_total, head_total, HD)
    key_heads = keys_here.reshape(key_total, head_total, HD)
    value_heads = values_here.reshape(key_total, head_total, HD)
    scores = jnp.einsum(
        "qhd,khd->hqk", query_heads, key_heads, preferred_element_type=jnp.float32
    ) * (1.0 / math.sqrt(HD))
    capped = logit_cap * jnp.tanh(scores / logit_cap)
    weights = jnp.exp(capped - logit_cap).astype(jnp.bfloat16)
    numerator = jnp.einsum("hqk,khd->qhd", weights, value_heads, preferred_element_type=jnp.float32)
    denominator = jnp.sum(weights, axis=-1, dtype=jnp.float32).T
    return (numerator.reshape(row_total, feature_width), denominator)


def body(span_q, span_k, span_v, q_gain, k_gain, kv_cache, frame_home, chosen_frames):
    query_float = span_q.astype(jnp.float32)
    key_float = span_k.astype(jnp.float32)
    query_square, key_square = lax.psum(
        (
            jnp.sum(query_float * query_float, axis=-1, keepdims=True),
            jnp.sum(key_float * key_float, axis=-1, keepdims=True),
        ),
        "heads",
    )
    query_local = (query_float * lax.rsqrt(query_square / D + 1e-06) * q_gain).astype(jnp.bfloat16)
    key_local = (key_float * lax.rsqrt(key_square / D + 1e-06) * k_gain).astype(jnp.bfloat16)
    locations = frame_home[chosen_frames]
    per_device = kv_cache.shape[0]
    bit_total = GROUP.bit_length() - 1
    bit_order = list(range(bit_total))
    numerator, denominator = partial_sums(query_local, key_local, span_v)
    stacked = jnp.stack([key_local, span_v])
    for section, bit in enumerate(bit_order):
        arrived = partner(stacked, "frames", bit)
        extra_terms = partial_sums(query_local, arrived[0], arrived[1])
        numerator = numerator + extra_terms[0]
        denominator = denominator + extra_terms[1]
        if section + 1 < len(bit_order):
            stacked = jnp.concatenate([stacked, arrived], axis=1)
    for which in range(SEL):
        location = locations[which]
        owner_index = location // per_device
        slot_index = location % per_device
        local_frame = lax.dynamic_index_in_dim(kv_cache, slot_index, 0, keepdims=False)
        fetched = from_root(local_frame, "frames", owner_index)
        extra_terms = partial_sums(query_local, fetched[0], fetched[1])
        numerator = numerator + extra_terms[0]
        denominator = denominator + extra_terms[1]
    row_total = numerator.shape[0]
    head_total = denominator.shape[1]
    attended = (numerator.reshape(row_total, head_total, HD) / denominator[:, :, None]).reshape(
        row_total, head_total * HD
    )
    return attended.astype(jnp.bfloat16)


def solution(mesh):
    placed = (
        P("frames", "heads"),
        P("frames", "heads"),
        P("frames", "heads"),
        P("heads"),
        P("heads"),
        P("frames", None, None, "heads"),
        P(),
        P(),
    )
    return jax.shard_map(
        body, mesh=mesh, in_specs=placed, out_specs=P("frames", "heads"), check_vma=False
    )
```

profile of v0, /device:TPU:2, one launch (start us, length us, event | category | flops | bytes accessed | tf_op | source)
XLA Modules:
  0.0 1257.1 jit_solution(11360366699956379290)
XLA Ops:
  6.5 1.6 copy.37
  8.2 0.3 fusion.3
  8.5 1.7 copy.36
  10.3 0.0 copy-start.18
  10.3 0.3 fusion
  10.6 1.7 copy.40
  12.3 5.8 all-reduce
  18.2 1.7 fusion.61
  19.9 0.2 pad_maximum_fusion.2
  20.1 0.0 copy-start.20
  20.1 2.1 collective-permute-start
  22.2 57.1 %collective-permute-done = bf16[2,512,1280]{1,2,0:T(8,128)(2,1)S(1)} collective-permute-done((bf16[2,512,1280]{1,2,0:T(8,128)(2,1)S(1)}, bf16[2,512,1280]{1,2,0:T(8,128)(2,1)S(1)}, u32[]{:S(2)}, u32[]{:S(2)}) %collective-permute-start) | collective-permute-done | bytes 2621472 | tf_op jit(solution)/shard_map/ppermute | solution.py:18
  79.3 3.2 pad_maximum_fusion.1
  82.6 2.8 collective-permute-start.1
  85.5 0.6 gather_fusion
  86.1 0.7 fusion.16
  99.9 3.6 constant_dynamic-slice_fusion.4
  103.5 2.2 copy.96
  105.7 2.2 copy.99
  107.9 2.2 copy.98
  110.0 2.2 copy.97
  112.2 1.1 copy.100
  113.3 0.9 select_bitcast_fusion.4
  114.2 0.9 select_bitcast_fusion.1
  115.1 0.9 select_bitcast_fusion.2
  116.0 0.9 select_bitcast_fusion.3
  116.9 0.9 select_bitcast_fusion
  117.8 0.0 all-reduce.4.cloned.1.call-update
  117.8 1.8 fusion.5
  119.7 208.0 %collective-permute-done.1 = bf16[2,1024,1280]{1,2,0:T(8,128)(2,1)} collective-permute-done((bf16[2,1024,1280]{1,2,0:T(8,128)(2,1)}, bf16[2,1024,1280]{1,2,0:T(8,128)(2,1)}, u32[]{:S(2)}, u32[]{:S(2)}) %collective-permute-start.1) | collective-permute-done | bytes 5242912 | tf_op jit(solution)/shard_map/ppermute | solution.py:18
  327.7 7.5 pad_maximum_fusion
  335.1 7.1 collective-permute-start.2
  342.2 0.4 fusion.2
  342.6 3.7 convert_reduce_fusion.3
  346.3 2.3 fusion.24
  348.6 0.2 fusion.10
  348.8 3.8 convert_reduce_fusion.2
  352.6 2.4 fusion.17
  355.0 813.4 %all-reduce.4.cloned.1.call-done = (bf16[2,128,1280]{1,2,0:T(8,128)(2,1)}, bf16[2,128,1280]{1,2,0:T(8,128)(2,1)}, bf16[2,128,1280]{1,2,0:T(8,128)(2,1)}, bf16[2,...) async-done(((bf16[2,128,1280]{1,2,0:T(8,128)(2,1)}, bf16[2,128,1280]{1,2,0:T(8,128)(2,1)}, bf16[2,128,1280]{1,2,0:T(8,128)(2,1)}, bf16[2,128,1280]{1,2,0:T(8,128)(2,1)}, ...) | async-done | bytes 3276816 | tf_op jit(solution)/shard_map/psum | solution.py:23
  1168.4 1.1 fusion.15
  1169.6 1.0 convert_reduce_fusion.4
  1170.6 0.1 copy-done.16
  1170.6 0.2 copy-done.17
  1170.8 0.1 fusion.13
  1170.9 1.0 convert_reduce_fusion.6
  1171.9 0.1 copy-done.14
  1172.0 0.2 copy-done.15
  1172.2 0.1 fusion.11
  1172.3 1.0 copy-done.13
  1173.3 1.0 convert_reduce_fusion.8
  1174.3 1.0 convert_reduce_fusion.7
  1175.3 1.0 convert_reduce_fusion.5
  1176.3 2.0 fusion.22
  1178.2 2.1 fusion.20
  1180.3 1.9 fusion.19
  1182.2 2.0 fusion.21
  1184.3 1.9 fusion.23
  1186.2 3.1 fusion.9
  1189.3 7.0 convert_reduce_fusion.1
  1196.3 5.1 fusion.18
  1201.5 10.2 fusion.8
  1211.6 19.3 %convert_reduce_fusion = (f32[10,512]{1,0:T(8,128)S(1)}, bf16[10,512,2048]{2,1,0:T(8,128)(2,1)}) fusion(bf16[512,10,128]{0,2,1:T(8,128)(2,1)} %bitcast.134, bf16[2048,10,128]{0,2,1:T(8,128)(2,1)} %bitcast.124), kind=kOutput, calls=%fused_computation.1 | convolution fusion | flops 2747264000 | bytes 27545600 | tf_op jit(solution)/shard_map/qhd,khd->hqk/dot_general | solution.py:34
  1231.0 16.9 %fusion.7 = bf16[512,10,128]{0,2,1:T(8,128)(2,1)} fusion(f32[10,128,512]{2,1,0:T(8,128)} %fusion.23, f32[10,128,512]{2,1,0:T(8,128)} %fusion.22, f32[10,128,512]{2,1,0:T(8,128)} %fusion.21, f32[10,128,512]{2,1,0:T(8,128)} %fusion.20, f32[10,128,512]{2,1,0:T(8,128)} %fusion.19, f32[10,128,512]{2,1,0:T(8,128)} %fusion.18, f32[10,128,512]{2,1,0:T(8,128)} %fusion.17, ...), kind=kOutput, calls=%fused_computation.24 | convolution fusion | flops 2690908160 | bytes 48517120 | tf_op jit(solution)/shard_map/hqk,khd->qhd/dot_general | solution.py:39
  1247.8 2.4 copy.70
  (41 shorter events, 0.1 us)
Async XLA Ops:
  6.5 78.9 %copy-start = (s32[128]{0:T(128)S(1)}, s32[128]{0:T(128)}, u32[]{:S(2)}) copy-start(s32[128]{0:T(128)} %param.14) | copy-start | bytes 1540
  6.5 1161.9 %all-reduce.4.cloned.1.call-start = ((), (), s32[]{:S(2)}) async-start(), calls=%async_computation | async-start | bytes 6553600 | tf_op jit(solution)/shard_map/psum | solution.py:23
  8.2 2.1 copy-start.4
  10.2 7.9 copy-start.6
  10.3 7.9 copy-start.18
  20.1 65.3 %copy-start.20 = (s32[5]{0:T(128)S(1)}, s32[5]{0:T(128)}, u32[]{:S(2)}) copy-start(s32[5]{0:T(128)} %param.15) | copy-start | bytes 64
  20.1 59.2 %collective-permute-start = (bf16[2,512,1280]{1,2,0:T(8,128)(2,1)S(1)}, bf16[2,512,1280]{1,2,0:T(8,128)(2,1)S(1)}, u32[]{:S(2)}, u32[]{:S(2)}) collective-permute-start(bf16[2,512,1280]{1,2,0:T(8,128)(2,1)S(1)} %pad_maximum_fusion.2), channel_id=1, source_target_pairs={{0,4},{4,0},{8,12},{12,8},{16,20},{20,16},{24,28},{28,24},{32,36},... | collective-permute-start | bytes 7864328 | tf_op jit(solution)/shard_map/ppermute | solution.py:18
  79.3 3.2 copy-start.2
  82.6 245.1 %collective-permute-start.1 = (bf16[2,1024,1280]{1,2,0:T(8,128)(2,1)}, bf16[2,1024,1280]{1,2,0:T(8,128)(2,1)}, u32[]{:S(2)}, u32[]{:S(2)}) collective-permute-start(bf16[2,1024,1280]{1,2,0:T(8,128)(2,1)} %pad_maximum_fusion.1), channel_id=1, source_target_pairs={{0,8},{4,12},{8,0},{12,4},{16,24},{20,28},{24,16},{28,20},{32,40},... | collective-permute-start | bytes 15728648 | tf_op jit(solution)/shard_map/ppermute | solution.py:18
  113.3 1.8 copy-start.10
  113.3 2.7 copy-start.8
  113.3 3.6 copy-start.9
  117.8 209.8 %copy-start.3 = (bf16[2,512,1280]{1,2,0:T(8,128)(2,1)S(1)}, bf16[2,512,1280]{1,2,0:T(8,128)(2,1)}, u32[]{:S(2)}) copy-start(bf16[2,512,1280]{1,2,0:T(8,128)(2,1)} %copy-done.2) | copy-start | bytes 7864324
  119.7 222.6 %copy-start.7 = (bf16[512,1280]{0,1:T(8,128)(2,1)S(1)}, bf16[512,1280]{0,1:T(8,128)(2,1)}, u32[]{:S(2)}) copy-start(bf16[512,1280]{0,1:T(8,128)(2,1)} %copy-done.6) | copy-start | bytes 3932164
  119.7 222.5 %copy-start.19 = (f32[1280]{0:T(1024)S(1)}, f32[1280]{0:T(1024)}, u32[]{:S(2)}) copy-start(f32[1280]{0:T(1024)} %param.11) | copy-start | bytes 15364
  335.1 866.3 %collective-permute-start.2 = (bf16[2,2048,1280]{1,2,0:T(8,128)(2,1)}, bf16[2,2048,1280]{1,2,0:T(8,128)(2,1)}, u32[]{:S(2)}, u32[]{:S(2)}) collective-permute-start(bf16[2,2048,1280]{1,2,0:T(8,128)(2,1)} %pad_maximum_fusion), channel_id=1, source_target_pairs={{0,16},{4,20},{8,24},{12,28},{16,0},{20,4},{24,8},{28,12},{32,48},... | collective-permute-start | bytes 31457288 | tf_op jit(solution)/shard_map/ppermute | solution.py:18
  342.6 6.2 copy-start.11
  352.6 816.9 %copy-start.12 = (bf16[512,1280]{0,1:T(8,128)(2,1)S(1)}, bf16[512,1280]{0,1:T(8,128)(2,1)}, u32[]{:S(2)}) copy-start(bf16[512,1280]{0,1:T(8,128)(2,1)} %copy-done.11) | copy-start | bytes 3932164
  1169.6 1.1 copy-start.16
  1169.6 1.3 copy-start.17
  1170.9 1.1 copy-start.14
  1170.9 1.3 copy-start.15
  1171.9 1.4 copy-start.13
  1211.6 19.3 %copy-start.5 = (f32[10,512,128]{1,2,0:T(8,128)S(1)}, f32[10,512,128]{1,2,0:T(8,128)}, u32[]{:S(2)}) copy-start(f32[10,512,128]{1,2,0:T(8,128)} %fusion.24) | copy-start | bytes 7864324
  1230.9 19.3 %copy-start.1 = (s32[128]{0:T(128)S(1)}, s32[128]{0:T(128)}, u32[]{:S(2)}) copy-start(s32[128]{0:T(128)} %param.14) | copy-start | bytes 1540
Sparse Core Ops, SparseCore 0:
  117.9 1050.4 all-reduce.3
where the time goes:
time: 1260 us
  waiting for transfers between devices  1080 us (86%)
  matrix products  75.3 us (6%)
  local copies, waits for them, and re-layouts  38.6 us (3%)
  between operations  26.8 us (2%)
  other arithmetic  20 us (2%)
    psum x1, waiting for transfers between devices, from_root(): return lax.psum(block, axis)  813 us
    ppermute x3, waiting for transfers between devices, partner(): lax.ppermute(value, axis, [(i, i ^ 1 << apart) for i in range(lax.axis_si...  265 us
    dot_general x9, matrix products, partial_sums(): jnp.einsum('qhd,khd->hqk', query_heads, key_heads, preferred_element_type...  38.7 us
    dot_general x9, matrix products, partial_sums(): jnp.einsum('hqk,khd->qhd', weights, value_heads, preferred_element_type=j...  36.6 us
  transfers between devices with their start and end apart: 4, of which 3 were waited for; matrix products, arithmetic and copies ran while one was open for 6% of the time, Pallas kernels for 0%

commit v1 on v0

v1 whole, which is shorter than its diff:
```python
import functools
import math

import jax
import jax.numpy as jnp
from jax import lax
from jax.experimental import pallas as pl
from jax.experimental.pallas import tpu as pltpu
from jax.sharding import Mesh, PartitionSpec as P

D = 5120
HD = 128
SEL = 5
CAND = 8
ZED = 8
GROUP = 4
MAIN = ZED * HD
CAP = 30.0
LOG2E = math.log2(math.e)
PARTS = (("m", 0, 128), ("m", 128, 128), ("l", 0, 128), ("m", 256, 128), ("m", 384, 128))


def attend_kernel(q_ref, k_ref, v_ref, kc_ref, vc_ref, o_ref):
    q = q_ref[...]
    total = None
    for keys, values in ((k_ref, v_ref), (kc_ref, vc_ref)):
        scores = lax.dot_general(
            q, keys[...], (((1,), (1,)), ((), ())), preferred_element_type=jnp.float32
        )
        capped = jnp.tanh(scores * (1.0 / (CAP * math.sqrt(HD))))
        weights = jnp.exp2(capped * (CAP * LOG2E) - CAP * LOG2E).astype(jnp.bfloat16)
        term = jnp.dot(weights, values[...], preferred_element_type=jnp.float32)
        total = term if total is None else total + term
    o_ref[...] = (total[:, :HD] / total[:, HD:]).astype(jnp.bfloat16)


def attend(q, k, v, kc, vc, block=512):
    rows, keys, cached = q.shape[0], k.shape[0], kc.shape[0]
    whole = lambda n, w: pl.BlockSpec((n, w), lambda i: (0, 0))
    return pl.pallas_call(
        attend_kernel,
        grid=(rows // block,),
        in_specs=[
            pl.BlockSpec((block, HD), lambda i: (i, 0)),
            whole(keys, HD),
            whole(keys, 2 * HD),
            whole(cached, HD),
            whole(cached, 2 * HD),
        ],
        out_specs=pl.BlockSpec((block, HD), lambda i: (i, 0)),
        out_shape=jax.ShapeDtypeStruct((rows, HD), jnp.bfloat16),
        compiler_params=pltpu.CompilerParams(vmem_limit_bytes=48 * 2**20),
        cost_estimate=pl.CostEstimate(
            flops=2 * rows * (keys + cached) * 3 * HD * 2,
            bytes_accessed=2 * (2 * rows + 3 * (keys + cached)) * HD,
            transcendentals=2 * rows * (keys + cached),
        ),
    )(q, k, v, kc, vc)


def to_heads(x):
    return lax.all_to_all(x, "z", 1, 0, tiled=True)


def with_ones(v):
    return jnp.concatenate([v, jnp.ones_like(v)], axis=1)


def cached_frames(kv_cache, locations):
    main = lax.all_to_all(kv_cache[..., :MAIN], "cand", 2, 0, tiled=True)
    left = lax.all_to_all(kv_cache[..., MAIN:], "h", 2, 3, tiled=True)
    left = lax.all_to_all(left, "cand", 2, 0, tiled=True)
    home = locations // 2
    slot = (home // ZED) * 2 + locations % 2
    mine = (home % ZED == lax.axis_index("z"))[:, None, None, None]
    pieces = []
    for part in (main, left):
        picked = jnp.stack([lax.dynamic_index_in_dim(part, slot[s], 0, keepdims=False) for s in range(SEL)])
        picked = jnp.where(mine, picked, jnp.zeros_like(picked))
        pieces.append(picked.reshape(-1, MAIN))
    rows = jnp.concatenate(pieces, axis=0)
    rows = rows.reshape(-1, ZED, HD).transpose(1, 0, 2)
    rows = lax.psum_scatter(rows, "z", scatter_dimension=0, tiled=True)[0]
    every = lax.all_gather(rows, "cand", axis=0)
    count = SEL * 2 * 16
    main = every[:, :count].reshape(CAND, SEL, 2, 16, HD)
    left = lax.all_gather(every[:, count:], "h", axis=0).reshape(GROUP, CAND, SEL, 2, 4, HD)
    return (
        main[:, :, 0].reshape(-1, HD),
        main[:, :, 1].reshape(-1, HD),
        left[:, :, :, 0].reshape(-1, HD),
        left[:, :, :, 1].reshape(-1, HD),
    )


def body(span_q, span_k, span_v, q_gain, k_gain, kv_cache, frame_home, chosen_frames):
    rows = span_q.shape[0]
    share = rows // GROUP
    v_main = to_heads(span_v[:, :MAIN])
    v_left = lax.all_to_all(span_v[:, MAIN:], "h", 0, 1, tiled=True)
    query_float = span_q.astype(jnp.float32)
    key_float = span_k.astype(jnp.float32)
    squares = jnp.stack(
        [jnp.sum(query_float * query_float, axis=-1), jnp.sum(key_float * key_float, axis=-1)]
    )
    squares = lax.psum(squares, "h")
    inverse = lax.rsqrt(squares / D + 1e-06)
    keys = (key_float * inverse[1][:, None] * k_gain).astype(jnp.bfloat16)
    queries = (query_float * inverse[0][:, None] * q_gain).astype(jnp.bfloat16)
    k_left = lax.all_to_all(keys[:, MAIN:], "h", 0, 1, tiled=True)
    q_left = lax.all_to_all(queries[:, MAIN:], "h", 0, 1, tiled=True)
    kv = to_heads(jnp.concatenate([keys[:, :MAIN], k_left, v_left], axis=0))
    kv = kv.reshape(ZED, rows + 2 * share, HD)
    k_main = kv[:, :rows].reshape(-1, HD)
    left = lax.all_gather(kv[:, rows:], "h", axis=0)
    k_rest = left[:, :, :share].reshape(-1, HD)
    v_rest = left[:, :, share:].reshape(-1, HD)
    kc_main, vc_main, kc_rest, vc_rest = cached_frames(kv_cache, frame_home[chosen_frames])

    main_side = (k_main, with_ones(v_main), kc_main, with_ones(vc_main))
    rest_side = (k_rest, with_ones(v_rest), kc_rest, with_ones(vc_rest))
    main_out = []
    for kind, first, count in PARTS:
        source = queries[:, :MAIN] if kind == "m" else q_left
        q = to_heads(source[first : first + count])
        out = attend(q, *(main_side if kind == "m" else rest_side))
        out = lax.all_to_all(out, "z", 0, 1, tiled=True)
        if kind == "m":
            main_out.append(out)
        else:
            rest_out = lax.all_to_all(out, "h", 1, 0, tiled=True)
    return jnp.concatenate([jnp.concatenate(main_out, axis=0), rest_out], axis=1)


def solution(mesh):
    grid = Mesh(mesh.devices.reshape(CAND, ZED, GROUP), ("cand", "z", "h"))
    tokens = P(("cand", "z"), "h")
    placed = (
        tokens,
        tokens,
        tokens,
        P("h"),
        P("h"),
        P(("cand", "z"), None, None, "h"),
        P(),
        P(),
    )
    return jax.shard_map(body, mesh=grid, in_specs=placed, out_specs=tokens, check_vma=False)
```

time: 1260 us -> 411 us (0.33)
  the two profiles are of different devices: /device:TPU:2 before, /device:TPU:1 now
where the time goes in v1:
time: 411 us; the launch traced here: 408 us
  waiting for transfers between devices  114 us (28%)
  starting transfers between devices  103 us (25%)
  local copies, waits for them, and re-layouts  55.5 us (14%)
  Pallas kernels  53.3 us (13%)
  blocking collectives  51.9 us (13%)
  between operations  24.9 us (6%)
  other arithmetic  6.27 us (2%)
    pallas_call x5, Pallas kernels, attend(): pl.pallas_call(attend_kernel, grid=(rows // block,), in_specs=[pl.BlockSp...  53.3 us
    unnamed x3, waiting for transfers between devices  36.7 us
    all_to_all x7, starting transfers between devices, to_heads(): return lax.all_to_all(x, 'z', 1, 0, tiled=True)  34.1 us
    all_to_all x7, waiting for transfers between devices, to_heads(): return lax.all_to_all(x, 'z', 1, 0, tiled=True)  33.7 us
    all_gather x1, blocking collectives, cached_frames(): every = lax.all_gather(rows, 'cand', axis=0)  30.7 us
    all_to_all x5, starting transfers between devices, body(): out = lax.all_to_all(out, 'z', 0, 1, tiled=True)  30.5 us
    unnamed x86, local copies, waits for them, and re-layouts  21.4 us
    all_gather x1, blocking collectives, cached_frames(): lax.all_gather(every[:, count:], 'h', axis=0)  15.9 us
  transfers between devices with their start and end apart: 21, of which 13 were waited for; matrix products, arithmetic and copies ran while one was open for 10% of the time, Pallas kernels for 13%

profile of v1, /device:TPU:1, one launch (start us, length us, event | category | flops | bytes accessed | tf_op | source)
XLA Modules:
  0.0 408.0 jit_solution(5505192185841407895)
XLA Ops:
  7.4 1.8 slice.102
  9.2 6.6 %all-to-all-start.2 = ((bf16[4,128,256]{2,1,0:T(8,128)(2,1)}), bf16[4,128,256]{2,1,0:T(8,128)(2,1)S(1)}, u32[]{:S(2)}, u32[]{:S(2)}) async-start(bf16[4,128,256]{2,1,0:T(8,128)(2,1)} %bitcast.9), calls=%async_computation.2 | async-start | bytes 524288 | tf_op jit(solution)/shard_map/all_to_all | solution.py:100
  15.8 1.7 fusion
  17.9 5.4 %psum.7 = f32[2,512]{1,0:T(2,128)S(1)} all-reduce(f32[2,512]{1,0:T(2,128)S(1)} %pad_maximum_fusion.2), channel_id=1, replica_groups=mesh['cand'=8,'z'=8,'h'=4] {'h'}, use_global_device_ids=true, to_apply=%region_2.0 | all-reduce | flops 1024 | bytes 8192 | tf_op jit(solution)/shard_map/psum | solution.py:106
  23.3 1.0 copy.99
  24.4 5.4 %all-to-all-start.6 = ((bf16[2,2,128,256]{3,1,0,2:T(2,128)(2,1)}), bf16[2,2,128,256]{3,1,0,2:T(2,128)(2,1)S(1)}, u32[]{:S(2)}, u32[]{:S(2)}) async-start(bf16[2,2,128,256]{3,1,0,2:T(2,128)(2,1)} %copy.99), calls=%async_computation.6 | async-start | bytes 524288 | tf_op jit(solution)/shard_map/all_to_all | solution.py:71
  30.1 1.1 copy-done.24
  32.0 3.0 all-to-all-done.6
  34.9 4.2 %all-to-all-start.15 = ((bf16[4,128,256]{2,1,0:T(8,128)(2,1)}), bf16[4,128,256]{2,1,0:T(8,128)(2,1)S(1)}, u32[]{:S(2)}, u32[]{:S(2)}) async-start(bf16[4,128,256]{2,1,0:T(8,128)(2,1)} %bitcast.49), calls=%async_computation.15 | async-start | bytes 524288 | tf_op jit(solution)/shard_map/all_to_all | solution.py:111
  39.6 1.0 copy-done.22
  41.4 3.0 all-to-all-done.15
  44.3 4.2 %all-to-all-start.1 = ((bf16[4,128,256]{2,1,0:T(8,128)(2,1)}), bf16[4,128,256]{2,1,0:T(8,128)(2,1)S(1)}, u32[]{:S(2)}, u32[]{:S(2)}) async-start(bf16[4,128,256]{2,1,0:T(8,128)(2,1)} %bitcast.6), calls=%async_computation.1 | async-start | bytes 524288 | tf_op jit(solution)/shard_map/all_to_all | solution.py:110
  49.0 1.0 copy.79
  50.0 3.8 all-to-all-done.1
  53.8 4.9 %all-to-all-start.7 = ((bf16[2,2,32,1024]{3,1,0,2:T(2,128)(2,1)}), bf16[2,2,32,1024]{3,1,0,2:T(2,128)(2,1)S(1)}, u32[]{:S(2)}, u32[]{:S(2)}) async-start(bf16[2,2,32,1024]{3,1,0,2:T(2,128)(2,1)} %copy.79), calls=%async_computation.7 | async-start | bytes 524288 | tf_op jit(solution)/shard_map/all_to_all | solution.py:72
  60.4 5.9 %all-to-all-done.7 = bf16[2,2,32,1024]{3,1,0,2:T(2,128)(2,1)S(1)} async-done(((bf16[2,2,32,1024]{3,1,0,2:T(2,128)(2,1)}), bf16[2,2,32,1024]{3,1,0,2:T(2,128)(2,1)S(1)}, u32[]{:S(2)}, u32[]{:S(2)}) %all-to-all-start.7) | async-done | bytes 262176 | tf_op jit(solution)/shard_map/all_to_all | solution.py:72
  66.3 8.2 %all-to-all-start = ((bf16[128,8,128]{2,0,1:T(8,128)(2,1)}), bf16[128,8,128]{2,0,1:T(8,128)(2,1)S(1)}, u32[]{:S(2)}, u32[]{:S(2)}) async-start(bf16[128,8,128]{2,0,1:T(8,128)(2,1)} %bitcast.127), calls=%async_computation | async-start | bytes 524288 | tf_op jit(solution)/shard_map/all_to_all | solution.py:62
  75.4 8.6 %all-to-all-done = bf16[128,8,128]{2,0,1:T(8,128)(2,1)S(1)} async-done(((bf16[128,8,128]{2,0,1:T(8,128)(2,1)}), bf16[128,8,128]{2,0,1:T(8,128)(2,1)S(1)}, u32[]{:S(2)}, u32[]{:S(2)}) %all-to-all-start) | async-done | bytes 262176 | tf_op jit(solution)/shard_map/all_to_all | solution.py:62
  83.9 3.4 all-to-all-start.16
  87.3 2.1 copy.98
  89.4 7.3 %all-to-all-done.16 = bf16[128,8,128]{0,2,1:T(8,128)(2,1)S(1)} async-done(((bf16[128,8,128]{0,2,1:T(8,128)(2,1)}), bf16[128,8,128]{0,2,1:T(8,128)(2,1)S(1)}, u32[]{:S(2)}, u32[]{:S(2)}) %all-to-all-start.16) | async-done | bytes 262176 | tf_op jit(solution)/shard_map/all_to_all | solution.py:62
  97.4 3.6 all-to-all-start.5
  101.0 2.5 copy_bitcast_fusion
  103.5 9.8 %all-to-all-done.5 = bf16[2,2,128,1024]{3,1,0,2:T(2,128)(2,1)S(1)} async-done(((bf16[2,2,128,1024]{3,1,0,2:T(2,128)(2,1)}), bf16[2,2,128,1024]{3,1,0,2:T(2,128)(2,1)S(1)}, u32[]{:S(2)}, u32[]{:S(2)}) %all-to-all-start.5) | async-done | bytes 1048608 | tf_op jit(solution)/shard_map/all_to_all | solution.py:70
  113.3 3.6 all-to-all-start.4
  128.2 1.1 copy.68
  129.5 1.2 copy.67
  130.9 1.3 pad_maximum_fusion
  132.3 9.6 %all-to-all-done.4 = bf16[512,8,128]{2,0,1:T(8,128)(2,1)S(1)} async-done(((bf16[512,8,128]{2,0,1:T(8,128)(2,1)}), bf16[512,8,128]{2,0,1:T(8,128)(2,1)S(1)}, u32[]{:S(2)}, u32[]{:S(2)}) %all-to-all-start.4) | async-done | bytes 1048608 | tf_op jit(solution)/shard_map/all_to_all | solution.py:62
  141.9 3.6 all-to-all-start.3
  145.8 1.5 copy.74
  148.6 1.7 copy.123
  150.3 1.7 copy.124
  152.0 1.7 copy.125
  153.7 1.8 copy.91
  155.5 36.6 %reduce-scatter.4.cloned.1.call-done = bf16[1,200,128]{2,1,0:T(8,128)(2,1)} async-done(((bf16[8,200,128]{2,1,0:T(8,128)(2,1)}), bf16[1,200,128]{2,1,0:T(8,128)(2,1)}) %reduce-scatter.4.cloned.1.call-update) | async-done | bytes 51216
  192.1 30.7 %all_gather.15 = bf16[8,200,128]{2,1,0:T(8,128)(2,1)S(1)} all-gather(bf16[1,200,128]{2,1,0:T(8,128)(2,1)} %reduce-scatter.4.cloned.1.call-done), channel_id=1, replica_groups=mesh['cand'=8,'z'=8,'h'=4] {'cand'}, dimensions={0}, use_global_device_ids=true | all-gather | bytes 460800 | tf_op jit(solution)/shard_map/all_gather | solution.py:84
  222.8 15.9 %all-gather.1 = bf16[32,40,128]{2,1,0:T(8,128)(2,1)S(1)} all-gather(bf16[8,40,128]{2,1,0:T(8,128)(2,1)S(1)} %slice.143), channel_id=3, replica_groups=mesh['cand'=8,'z'=8,'h'=4] {'h'}, dimensions={0}, use_global_device_ids=true | all-gather | bytes 409600 | tf_op jit(solution)/shard_map/all_gather | solution.py:87
  238.8 4.8 %all-to-all-start.13 = ((bf16[128,8,128]{2,0,1:T(8,128)(2,1)}), bf16[128,8,128]{2,0,1:T(8,128)(2,1)}, u32[]{:S(2)}, u32[]{:S(2)}) async-start(bf16[128,8,128]{2,0,1:T(8,128)(2,1)} %bitcast.167), calls=%async_computation.13 | async-start | bytes 524288 | tf_op jit(solution)/shard_map/all_to_all | solution.py:62
  247.7 8.3 %all-to-all-done.13 = bf16[128,8,128]{2,0,1:T(8,128)(2,1)} async-done(((bf16[128,8,128]{2,0,1:T(8,128)(2,1)}), bf16[128,8,128]{2,0,1:T(8,128)(2,1)}, u32[]{:S(2)}, u32[]{:S(2)}) %all-to-all-start.13) | async-done | bytes 262176 | tf_op jit(solution)/shard_map/all_to_all | solution.py:62
  255.9 4.2 %all-to-all-start.9 = ((bf16[128,8,128]{2,0,1:T(8,128)(2,1)}), bf16[128,8,128]{2,0,1:T(8,128)(2,1)}, u32[]{:S(2)}, u32[]{:S(2)}) async-start(bf16[128,8,128]{2,0,1:T(8,128)(2,1)} %bitcast.166), calls=%async_computation.9 | async-start | bytes 524288 | tf_op jit(solution)/shard_map/all_to_all | solution.py:62
  262.1 11.0 %shard_map.85 = bf16[1024,128]{1,0:T(8,128)(2,1)S(1)} custom-call(bf16[1024,128]{1,0:T(8,128)(2,1)} %bitcast.46.q_ref, bf16[4096,128]{1,0:T(8,128)(2,1)S(1)} %bitcast.129, bf16[4096,256]{1,0:T(8,128)(2,1)S(1)} %concatenate.36.v_ref, bf16[640,128]{1,0:T(8,128)(2,1)S(1)} %bitcast.141, bf16[640,256]{1,0:T(8,128)(2,1)S(1)} %copy-done.1), custom_call_target="tpu_custom_call" | custom-call | flops 7449083904 | bytes 4161536 | tf_op jit(solution)/shard_map/pallas_call | solution.py:40
  273.8 6.4 %all-to-all-start.11 = ((bf16[128,8,128]{2,0,1:T(8,128)(2,1)}), bf16[128,8,128]{2,0,1:T(8,128)(2,1)}, u32[]{:S(2)}, u32[]{:S(2)}) async-start(bf16[128,8,128]{2,0,1:T(8,128)(2,1)} %bitcast.165), calls=%async_computation.11 | async-start | bytes 524288 | tf_op jit(solution)/shard_map/all_to_all | solution.py:62
  280.2 1.0 copy-done.2
  282.1 11.0 %shard_map.83 = bf16[1024,128]{1,0:T(8,128)(2,1)S(1)} custom-call(bf16[1024,128]{1,0:T(8,128)(2,1)} %bitcast.38.q_ref, bf16[4096,128]{1,0:T(8,128)(2,1)S(1)} %bitcast.130, bf16[4096,256]{1,0:T(8,128)(2,1)S(1)} %concatenate.36.v_ref, bf16[640,128]{1,0:T(8,128)(2,1)S(1)} %bitcast.142, bf16[640,256]{1,0:T(8,128)(2,1)S(1)} %copy-done.2), custom_call_target="tpu_custom_call" | custom-call | flops 7449083904 | bytes 4161536 | tf_op jit(solution)/shard_map/pallas_call | solution.py:40
  293.8 6.6 %all-to-all-start.10 = ((bf16[8,128,128]{2,1,0:T(8,128)(2,1)}), bf16[8,128,128]{2,1,0:T(8,128)(2,1)}, u32[]{:S(2)}, u32[]{:S(2)}) async-start(bf16[8,128,128]{2,1,0:T(8,128)(2,1)} %bitcast.139), calls=%async_computation.10 | async-start | bytes 524288 | tf_op jit(solution)/shard_map/all_to_all | solution.py:127
  303.3 10.1 %shard_map.82 = bf16[1024,128]{1,0:T(8,128)(2,1)S(1)} custom-call(bf16[1024,128]{1,0:T(8,128)(2,1)S(1)} %bitcast.134, bf16[4096,128]{1,0:T(8,128)(2,1)S(1)} %bitcast.131, bf16[4096,256]{1,0:T(8,128)(2,1)S(1)} %concatenate.36.v_ref, bf16[640,128]{1,0:T(8,128)(2,1)S(1)} %bitcast.143, bf16[640,256]{1,0:T(8,128)(2,1)S(1)} %copy-done.3), custom_call_target="tpu_custom_call" | custom-call | flops 7449083904 | bytes 4161536 | tf_op jit(solution)/shard_map/pallas_call | solution.py:40
  314.1 6.6 %all-to-all-start.8 = ((bf16[8,128,128]{2,1,0:T(8,128)(2,1)}), bf16[8,128,128]{2,1,0:T(8,128)(2,1)}, u32[]{:S(2)}, u32[]{:S(2)}) async-start(bf16[8,128,128]{2,1,0:T(8,128)(2,1)} %bitcast.138), calls=%async_computation.8 | async-start | bytes 524288 | tf_op jit(solution)/shard_map/all_to_all | solution.py:127
  322.6 11.0 %shard_map.84 = bf16[1024,128]{1,0:T(8,128)(2,1)S(1)} custom-call(bf16[1024,128]{1,0:T(8,128)(2,1)} %bitcast.42.q_ref, bf16[4096,128]{1,0:T(8,128)(2,1)S(1)} %bitcast.132, bf16[4096,256]{1,0:T(8,128)(2,1)S(1)} %concatenate.36.v_ref, bf16[640,128]{1,0:T(8,128)(2,1)S(1)} %bitcast.144, bf16[640,256]{1,0:T(8,128)(2,1)S(1)} %copy-done.4), custom_call_target="tpu_custom_call" | custom-call | flops 7449083904 | bytes 4161536 | tf_op jit(solution)/shard_map/pallas_call | solution.py:40
  334.4 6.6 %all-to-all-start.12 = ((bf16[8,128,128]{2,1,0:T(8,128)(2,1)}), bf16[8,128,128]{2,1,0:T(8,128)(2,1)}, u32[]{:S(2)}, u32[]{:S(2)}) async-start(bf16[8,128,128]{2,1,0:T(8,128)(2,1)} %bitcast.137), calls=%async_computation.12 | async-start | bytes 524288 | tf_op jit(solution)/shard_map/all_to_all | solution.py:127
  341.0 1.7 copy_bitcast_fusion.4
  342.7 1.7 fusion.8
  344.6 5.9 %all-to-all-done.12 = bf16[8,128,128]{2,1,0:T(8,128)(2,1)} async-done(((bf16[8,128,128]{2,1,0:T(8,128)(2,1)}), bf16[8,128,128]{2,1,0:T(8,128)(2,1)}, u32[]{:S(2)}, u32[]{:S(2)}) %all-to-all-start.12) | async-done | bytes 262176 | tf_op jit(solution)/shard_map/all_to_all | solution.py:127
  350.5 4.3 %all-to-all-start.14 = ((bf16[8,128,128]{2,1,0:T(8,128)(2,1)}), bf16[8,128,128]{2,1,0:T(8,128)(2,1)}, u32[]{:S(2)}, u32[]{:S(2)}) async-start(bf16[8,128,128]{2,1,0:T(8,128)(2,1)} %bitcast.136), calls=%async_computation.14 | async-start | bytes 524288 | tf_op jit(solution)/shard_map/all_to_all | solution.py:127
  356.7 10.1 %shard_map.86 = bf16[1024,128]{1,0:T(8,128)(2,1)S(1)} custom-call(bf16[1024,128]{1,0:T(8,128)(2,1)S(1)} %bitcast.135, bf16[4096,128]{1,0:T(8,128)(2,1)S(1)} %bitcast.133, bf16[4096,256]{1,0:T(8,128)(2,1)S(1)} %concatenate.40.v_ref, bf16[640,128]{1,0:T(8,128)(2,1)S(1)} %bitcast.145, bf16[640,256]{1,0:T(8,128)(2,1)S(1)} %concatenate.41.vc_ref), custom_call_target="tpu_custom_call" | custom-call | flops 7449083904 | bytes 4161536 | tf_op jit(solution)/shard_map/pallas_call | solution.py:40
  367.5 1.8 copy.95
  369.4 6.3 %all-to-all-start.17 = ((bf16[8,128,128]{1,2,0:T(8,128)(2,1)}), bf16[8,128,128]{1,2,0:T(8,128)(2,1)}, u32[]{:S(2)}, u32[]{:S(2)}) async-start(bf16[8,128,128]{1,2,0:T(8,128)(2,1)} %copy.95), calls=%async_computation.17 | async-start | bytes 524288 | tf_op jit(solution)/shard_map/all_to_all | solution.py:127
  375.7 1.0 copy_bitcast_fusion.5
  376.6 1.0 copy_bitcast_fusion.3
  377.6 7.6 %all-to-all-done.17 = bf16[8,128,128]{1,2,0:T(8,128)(2,1)} async-done(((bf16[8,128,128]{1,2,0:T(8,128)(2,1)}), bf16[8,128,128]{1,2,0:T(8,128)(2,1)}, u32[]{:S(2)}, u32[]{:S(2)}) %all-to-all-start.17) | async-done | bytes 262176 | tf_op jit(solution)/shard_map/all_to_all | solution.py:127
  385.2 8.9 %all-to-all-start.18 = ((bf16[128,4,256]{0,2,1:T(8,128)(2,1)}), bf16[128,4,256]{0,2,1:T(8,128)(2,1)S(1)}, u32[]{:S(2)}, u32[]{:S(2)}) async-start(bf16[128,4,256]{0,2,1:T(8,128)(2,1)} %bitcast.62), calls=%async_computation.18 | async-start | bytes 524288 | tf_op jit(solution)/shard_map/all_to_all | solution.py:131
  394.1 1.0 copy_bitcast_fusion.2
  395.0 4.2 %all-to-all-done.18 = bf16[128,4,256]{0,2,1:T(8,128)(2,1)S(1)} async-done(((bf16[128,4,256]{0,2,1:T(8,128)(2,1)}), bf16[128,4,256]{0,2,1:T(8,128)(2,1)S(1)}, u32[]{:S(2)}, u32[]{:S(2)}) %all-to-all-start.18) | async-done | bytes 262176 | tf_op jit(solution)/shard_map/all_to_all | solution.py:131
  399.4 1.1 pad_maximum_fusion.1
  (145 shorter events, 27.5 us)
Async XLA Ops:
  7.4 109.5 %copy-start = (s32[128]{0:T(128)S(1)}, s32[128]{0:T(128)}, u32[]{:S(2)}) copy-start(s32[128]{0:T(128)} %param.14) | copy-start | bytes 1540
  7.4 10.2 %copy-start.21 = (bf16[512,1280]{1,0:T(8,128)(2,1)S(1)}, bf16[512,1280]{1,0:T(8,128)(2,1)}, u32[]{:S(2)}) copy-start(bf16[512,1280]{1,0:T(8,128)(2,1)} %param.9) | copy-start | bytes 3932164
  7.4 16.0 %slice-start = ((bf16[2,2,128,1280]{3,2,1,0:T(8,128)(2,1)}), bf16[2,2,128,256]{3,2,1,0:T(8,128)(2,1)S(1)}, s32[]{:S(2)}) async-start(bf16[2,2,128,1280]{3,2,1,0:T(8,128)(2,1)} %param.13), calls=%async_computation.22 | async-start | bytes 524288 | tf_op jit(solution)/shard_map/slice | solution.py:71
  9.2 15.2 %all-to-all-start.2 = ((bf16[4,128,256]{2,1,0:T(8,128)(2,1)}), bf16[4,128,256]{2,1,0:T(8,128)(2,1)S(1)}, u32[]{:S(2)}, u32[]{:S(2)}) async-start(bf16[4,128,256]{2,1,0:T(8,128)(2,1)} %bitcast.9), calls=%async_computation.2 | async-start | bytes 524288 | tf_op jit(solution)/shard_map/all_to_all | solution.py:100
  15.8 14.0 %copy-start.20 = (bf16[512,1280]{1,0:T(8,128)(2,1)S(1)}, bf16[512,1280]{1,0:T(8,128)(2,1)}, u32[]{:S(2)}) copy-start(bf16[512,1280]{1,0:T(8,128)(2,1)} %param.8) | copy-start | bytes 3932164
  15.8 14.0 %copy-start.34 = (f32[1280]{0:T(1024)S(1)}, f32[1280]{0:T(1024)}, u32[]{:S(2)}) copy-start(f32[1280]{0:T(1024)} %param.11) | copy-start | bytes 15364
  24.3 14.8 %copy-start.35 = (f32[1280]{0:T(1024)S(1)}, f32[1280]{0:T(1024)}, u32[]{:S(2)}) copy-start(f32[1280]{0:T(1024)} %param.12) | copy-start | bytes 15364
  24.3 10.6 %copy-start.28 = (bf16[4,128,256]{2,1,0:T(8,128)(2,1)}, bf16[4,128,256]{2,1,0:T(8,128)(2,1)S(1)}, u32[]{:S(2)}) copy-start(bf16[4,128,256]{2,1,0:T(8,128)(2,1)S(1)} %all-to-all-done.2) | copy-start | bytes 786436
  24.4 10.6 %all-to-all-start.6 = ((bf16[2,2,128,256]{3,1,0,2:T(2,128)(2,1)}), bf16[2,2,128,256]{3,1,0,2:T(2,128)(2,1)S(1)}, u32[]{:S(2)}, u32[]{:S(2)}) async-start(bf16[2,2,128,256]{3,1,0,2:T(2,128)(2,1)} %copy.99), calls=%async_computation.6 | async-start | bytes 524288 | tf_op jit(solution)/shard_map/all_to_all | solution.py:71
  30.1 1.1 copy-start.24
  34.9 9.4 %all-to-all-start.15 = ((bf16[4,128,256]{2,1,0:T(8,128)(2,1)}), bf16[4,128,256]{2,1,0:T(8,128)(2,1)S(1)}, u32[]{:S(2)}, u32[]{:S(2)}) async-start(bf16[4,128,256]{2,1,0:T(8,128)(2,1)} %bitcast.49), calls=%async_computation.15 | async-start | bytes 524288 | tf_op jit(solution)/shard_map/all_to_all | solution.py:111
  39.5 1.1 copy-start.22
  40.6 18.1 %copy-start.25 = (bf16[512,1280]{1,0:T(8,128)(2,1)S(1)}, bf16[512,1280]{1,0:T(8,128)(2,1)}, u32[]{:S(2)}) copy-start(bf16[512,1280]{1,0:T(8,128)(2,1)} %copy-done.24) | copy-start | bytes 3932164
  44.3 9.4 %all-to-all-start.1 = ((bf16[4,128,256]{2,1,0:T(8,128)(2,1)}), bf16[4,128,256]{2,1,0:T(8,128)(2,1)S(1)}, u32[]{:S(2)}, u32[]{:S(2)}) async-start(bf16[4,128,256]{2,1,0:T(8,128)(2,1)} %bitcast.6), calls=%async_computation.1 | async-start | bytes 524288 | tf_op jit(solution)/shard_map/all_to_all | solution.py:110
  53.8 21.6 %copy-start.30 = (bf16[4,128,256]{2,1,0:T(8,128)(2,1)}, bf16[4,128,256]{2,1,0:T(8,128)(2,1)S(1)}, u32[]{:S(2)}) copy-start(bf16[4,128,256]{2,1,0:T(8,128)(2,1)S(1)} %all-to-all-done.1) | copy-start | bytes 786436
  53.8 12.6 %all-to-all-start.7 = ((bf16[2,2,32,1024]{3,1,0,2:T(2,128)(2,1)}), bf16[2,2,32,1024]{3,1,0,2:T(2,128)(2,1)S(1)}, u32[]{:S(2)}, u32[]{:S(2)}) async-start(bf16[2,2,32,1024]{3,1,0,2:T(2,128)(2,1)} %copy.79), calls=%async_computation.7 | async-start | bytes 524288 | tf_op jit(solution)/shard_map/all_to_all | solution.py:72
  59.6 27.7 %slice-start.1 = ((bf16[2,2,128,1280]{3,2,1,0:T(8,128)(2,1)}), bf16[2,2,128,1024]{3,2,1,0:T(8,128)(2,1)S(1)}, s32[]{:S(2)}) async-start(bf16[2,2,128,1280]{3,2,1,0:T(8,128)(2,1)} %param.13), calls=%async_computation.23 | async-start | bytes 2097152 | tf_op jit(solution)/shard_map/slice | solution.py:70
  66.3 23.1 %copy-start.31 = (bf16[2,2,32,1024]{3,1,0,2:T(2,128)(2,1)}, bf16[2,2,32,1024]{3,1,0,2:T(2,128)(2,1)S(1)}, u32[]{:S(2)}) copy-start(bf16[2,2,32,1024]{3,1,0,2:T(2,128)(2,1)S(1)} %all-to-all-done.7) | copy-start | bytes 786436
  66.3 17.6 %all-to-all-start = ((bf16[128,8,128]{2,0,1:T(8,128)(2,1)}), bf16[128,8,128]{2,0,1:T(8,128)(2,1)S(1)}, u32[]{:S(2)}, u32[]{:S(2)}) async-start(bf16[128,8,128]{2,0,1:T(8,128)(2,1)} %bitcast.127), calls=%async_computation | async-start | bytes 524288 | tf_op jit(solution)/shard_map/all_to_all | solution.py:62
  83.9 5.5 %copy-start.5 = (bf16[128,8,128]{2,0,1:T(8,128)(2,1)}, bf16[128,8,128]{2,0,1:T(8,128)(2,1)S(1)}, u32[]{:S(2)}) copy-start(bf16[128,8,128]{2,0,1:T(8,128)(2,1)S(1)} %all-to-all-done) | copy-start | bytes 786436
  83.9 12.8 %all-to-all-start.16 = ((bf16[128,8,128]{0,2,1:T(8,128)(2,1)}), bf16[128,8,128]{0,2,1:T(8,128)(2,1)S(1)}, u32[]{:S(2)}, u32[]{:S(2)}) async-start(bf16[128,8,128]{0,2,1:T(8,128)(2,1)} %bitcast.51), calls=%async_computation.16 | async-start | bytes 524288 | tf_op jit(solution)/shard_map/all_to_all | solution.py:62
  96.7 0.7 copy-start.29
  97.4 15.8 %all-to-all-start.5 = ((bf16[2,2,128,1024]{3,1,0,2:T(2,128)(2,1)}), bf16[2,2,128,1024]{3,1,0,2:T(2,128)(2,1)S(1)}, u32[]{:S(2)}, u32[]{:S(2)}) async-start(bf16[2,2,128,1024]{3,1,0,2:T(2,128)(2,1)} %copy.98), calls=%async_computation.5 | async-start | bytes 2097152 | tf_op jit(solution)/shard_map/all_to_all | solution.py:70
  101.0 15.8 %copy-start.36 = (s32[5]{0:T(128)S(1)}, s32[5]{0:T(128)}, u32[]{:S(2)}) copy-start(s32[5]{0:T(128)} %param.15) | copy-start | bytes 64
  101.0 27.0 %copy-start.23 = (bf16[512,1280]{1,0:T(8,128)(2,1)S(1)}, bf16[512,1280]{1,0:T(8,128)(2,1)}, u32[]{:S(2)}) copy-start(bf16[512,1280]{1,0:T(8,128)(2,1)} %copy-done.22) | copy-start | bytes 3932164
  113.3 14.1 %copy-start.26 = (bf16[2,2,128,1024]{3,1,0,2:T(2,128)(2,1)}, bf16[2,2,128,1024]{3,1,0,2:T(2,128)(2,1)S(1)}, u32[]{:S(2)}) copy-start(bf16[2,2,128,1024]{3,1,0,2:T(2,128)(2,1)S(1)} %all-to-all-done.5) | copy-start | bytes 3145732
  113.3 28.6 %all-to-all-start.4 = ((bf16[512,8,128]{2,0,1:T(8,128)(2,1)}), bf16[512,8,128]{2,0,1:T(8,128)(2,1)S(1)}, u32[]{:S(2)}, u32[]{:S(2)}) async-start(bf16[512,8,128]{2,0,1:T(8,128)(2,1)} %copy_bitcast_fusion), calls=%async_computation.4 | async-start | bytes 2097152 | tf_op jit(solution)/shard_map/all_to_all | solution.py:62
  129.5 2.6 copy-start.32
  141.9 96.9 %all-to-all-start.3 = ((bf16[768,8,128]{2,0,1:T(8,128)(2,1)}), bf16[768,8,128]{2,0,1:T(8,128)(2,1)S(1)}, u32[]{:S(2)}, u32[]{:S(2)}) async-start(bf16[768,8,128]{2,0,1:T(8,128)(2,1)} %pad_maximum_fusion), calls=%async_computation.3 | async-start | bytes 3145728 | tf_op jit(solution)/shard_map/all_to_all | solution.py:62
  145.5 46.6 %reduce-scatter.4.cloned.1.call-start = ((), (), s32[]{:S(2)}) async-start(), calls=%async_computation.21 | async-start | bytes 460800
  238.8 7.4 %copy-start.18 = (bf16[768,8,128]{2,0,1:T(8,128)(2,1)}, bf16[768,8,128]{2,0,1:T(8,128)(2,1)S(1)}, u32[]{:S(2)}) copy-start(bf16[768,8,128]{2,0,1:T(8,128)(2,1)S(1)} %all-to-all-done.3) | copy-start | bytes 4718596
  238.8 17.2 %all-to-all-start.13 = ((bf16[128,8,128]{2,0,1:T(8,128)(2,1)}), bf16[128,8,128]{2,0,1:T(8,128)(2,1)}, u32[]{:S(2)}, u32[]{:S(2)}) async-start(bf16[128,8,128]{2,0,1:T(8,128)(2,1)} %bitcast.167), calls=%async_computation.13 | async-start | bytes 524288 | tf_op jit(solution)/shard_map/all_to_all | solution.py:62
  243.6 99.1 %all-gather.4.cloned.1.call-start = ((), (), s32[]{:S(2)}) async-start(), calls=%async_computation.20 | async-start | bytes 2621440 | tf_op jit(solution)/shard_map/all_gather | solution.py:115
  244.4 1.0 copy-start.33
  246.1 1.5 copy-start.19
  255.9 17.9 %all-to-all-start.9 = ((bf16[128,8,128]{2,0,1:T(8,128)(2,1)}), bf16[128,8,128]{2,0,1:T(8,128)(2,1)}, u32[]{:S(2)}, u32[]{:S(2)}) async-start(bf16[128,8,128]{2,0,1:T(8,128)(2,1)} %bitcast.166), calls=%async_computation.9 | async-start | bytes 524288 | tf_op jit(solution)/shard_map/all_to_all | solution.py:62
  260.2 1.0 copy-start.1
  261.2 0.9 copy-start.13
  273.1 0.7 copy-start.8
  273.8 20.0 %all-to-all-start.11 = ((bf16[128,8,128]{2,0,1:T(8,128)(2,1)}), bf16[128,8,128]{2,0,1:T(8,128)(2,1)}, u32[]{:S(2)}, u32[]{:S(2)}) async-start(bf16[128,8,128]{2,0,1:T(8,128)(2,1)} %bitcast.165), calls=%async_computation.11 | async-start | bytes 524288 | tf_op jit(solution)/shard_map/all_to_all | solution.py:62
  280.2 1.0 copy-start.2
  281.2 0.9 copy-start.14
  293.1 0.7 copy-start.11
  293.8 20.3 %all-to-all-start.10 = ((bf16[8,128,128]{2,1,0:T(8,128)(2,1)}), bf16[8,128,128]{2,1,0:T(8,128)(2,1)}, u32[]{:S(2)}, u32[]{:S(2)}) async-start(bf16[8,128,128]{2,1,0:T(8,128)(2,1)} %bitcast.139), calls=%async_computation.10 | async-start | bytes 524288 | tf_op jit(solution)/shard_map/all_to_all | solution.py:127
  300.5 1.0 copy-start.3
  301.4 0.9 copy-start.6
  302.4 0.9 copy-start.15
  313.4 0.7 copy-start.10
  314.1 20.3 %all-to-all-start.8 = ((bf16[8,128,128]{2,1,0:T(8,128)(2,1)}), bf16[8,128,128]{2,1,0:T(8,128)(2,1)}, u32[]{:S(2)}, u32[]{:S(2)}) async-start(bf16[8,128,128]{2,1,0:T(8,128)(2,1)} %bitcast.138), calls=%async_computation.8 | async-start | bytes 524288 | tf_op jit(solution)/shard_map/all_to_all | solution.py:127
  320.8 1.0 copy-start.4
  321.7 0.9 copy-start.16
  333.7 0.7 copy-start.9
  334.4 16.2 %all-to-all-start.12 = ((bf16[8,128,128]{2,1,0:T(8,128)(2,1)}), bf16[8,128,128]{2,1,0:T(8,128)(2,1)}, u32[]{:S(2)}, u32[]{:S(2)}) async-start(bf16[8,128,128]{2,1,0:T(8,128)(2,1)} %bitcast.137), calls=%async_computation.12 | async-start | bytes 524288 | tf_op jit(solution)/shard_map/all_to_all | solution.py:127
  350.5 18.8 %all-to-all-start.14 = ((bf16[8,128,128]{2,1,0:T(8,128)(2,1)}), bf16[8,128,128]{2,1,0:T(8,128)(2,1)}, u32[]{:S(2)}, u32[]{:S(2)}) async-start(bf16[8,128,128]{2,1,0:T(8,128)(2,1)} %bitcast.136), calls=%async_computation.14 | async-start | bytes 524288 | tf_op jit(solution)/shard_map/all_to_all | solution.py:127
  354.9 1.0 copy-start.7
  355.8 0.9 copy-start.17
  366.8 0.7 copy-start.12
  367.5 31.9 %copy-start.27 = (bf16[128,1024]{1,0:T(8,128)(2,1)S(1)}, bf16[128,1024]{1,0:T(8,128)(2,1)}, u32[]{:S(2)}) copy-start(bf16[128,1024]{1,0:T(8,128)(2,1)} %copy_bitcast_fusion.4) | copy-start | bytes 786436
  369.4 15.8 %all-to-all-start.17 = ((bf16[8,128,128]{1,2,0:T(8,128)(2,1)}), bf16[8,128,128]{1,2,0:T(8,128)(2,1)}, u32[]{:S(2)}, u32[]{:S(2)}) async-start(bf16[8,128,128]{1,2,0:T(8,128)(2,1)} %copy.95), calls=%async_computation.17 | async-start | bytes 524288 | tf_op jit(solution)/shard_map/all_to_all | solution.py:127
  385.2 14.0 %all-to-all-start.18 = ((bf16[128,4,256]{0,2,1:T(8,128)(2,1)}), bf16[128,4,256]{0,2,1:T(8,128)(2,1)S(1)}, u32[]{:S(2)}, u32[]{:S(2)}) async-start(bf16[128,4,256]{0,2,1:T(8,128)(2,1)} %bitcast.62), calls=%async_computation.18 | async-start | bytes 524288 | tf_op jit(solution)/shard_map/all_to_all | solution.py:131
Sparse Core Ops, SparseCore 0:
  148.9 43.2 reduce-scatter.3
Sparse Core Ops, SparseCore 1:
  245.9 31.4 all-gather.3
